TPU v7x, 512 devices: a whole 4x8x8 slice. The times are simulated.
512 devices in a mesh: chan: 16 (over y_lo, z), frame: 32 (over x, y_hi, core).
Axes of the slice: x: 4, y: 8 (y_hi: 4, y_lo: 2; y = y_hi * 2 + y_lo), z: 8, core: 2. Of those that a mesh axis runs over, the one named last changes fastest.
Arguments:
- images: float32 [64, 32, 2, 256, 256], P('chan', 'frame'), may hold values from -6 to 6
- objects: float32 [64, 2, 256, 256], P('chan', None, 'frame'), may hold values from -24 to 24
- coeffs: float32 [32, 36], P('frame'), may hold values from -0.875 to 0.875
- mode_maps: float32 [36, 128, 128], P(None, 'chan'), may hold values from -4 to 4
- amplitude: float32 [128, 128], replicated, may hold values from 0.5 to 1.5
- phase_scale: float32 [64], P('chan'), may hold values from 0.6 to 1.2
Outputs:
- obj_grad: float32 [64, 2, 256, 256], P('chan', None, 'frame')
- mode_grad: float32 [32, 36], P('frame')
All inputs are finite; a program needn't handle non-finite values.
Results may differ from a plain program's by a relative error of at most 0.0001.
Values sent between devices are 32-bit elements; how exact they have to be, the bound alone decides.
A program may use at most 64 MiB of HBM per device.

v0:
```python
import math

import jax
import jax.numpy as jnp
from jax import lax
from jax.sharding import PartitionSpec as P

HIGHEST = lax.Precision.HIGHEST


def circle_mask(extent):
    row_index = lax.broadcasted_iota(jnp.int32, (extent, extent), 0).astype(jnp.float32)
    col_index = lax.broadcasted_iota(jnp.int32, (extent, extent), 1).astype(jnp.float32)
    centre = (extent - 1) / 2.0
    radius = extent / 2.0
    inside = (row_index - centre) ** 2 + (col_index - centre) ** 2 <= radius * radius
    return jnp.where(inside, 1.0, 0.0).astype(jnp.float32)


def dft_table(extent, columns):
    row_index = lax.broadcasted_iota(jnp.int32, (extent, columns), 0)
    col_index = lax.broadcasted_iota(jnp.int32, (extent, columns), 1)
    turn_angle = (row_index * col_index % extent).astype(jnp.float32) * (2.0 * math.pi / extent)
    return (jnp.cos(turn_angle), -jnp.sin(turn_angle))


def contract(pattern, left_side, right_side):
    return jnp.einsum(
        pattern, left_side, right_side, precision=HIGHEST, preferred_element_type=jnp.float32
    )


def right_apply(real_part, imag_part, table_real, table_imag):
    pattern = "cfxy,yv->cfxv"
    out_real = contract(pattern, real_part, table_real) - contract(pattern, imag_part, table_imag)
    out_imag = contract(pattern, real_part, table_imag) + contract(pattern, imag_part, table_real)
    return (out_real, out_imag)


def left_apply(table_real, table_imag, real_part, imag_part):
    pattern = "ux,cfxv->cfuv"
    out_real = contract(pattern, table_real, real_part) - contract(pattern, table_imag, imag_part)
    out_imag = contract(pattern, table_imag, real_part) + contract(pattern, table_real, imag_part)
    return (out_real, out_imag)


def on_device(images, objects, coeffs, mode_maps, amplitude, phase_scale):
    grid_size = images.shape[-1]
    pupil_size = amplitude.shape[0]
    aperture = amplitude * circle_mask(pupil_size)
    psf_norm = grid_size * grid_size * jnp.sum(aperture * aperture)
    full_maps = lax.all_gather(mode_maps, "chan", axis=1, tiled=True)
    phases = contract("fm,mxy->fxy", coeffs, full_maps)
    gathered = lax.all_gather(objects, "frame", axis=2, tiled=True)
    wide_real, wide_imag = dft_table(grid_size, pupil_size)
    full_real, full_imag = dft_table(grid_size, grid_size)
    angles = phase_scale[:, None, None, None] * phases[None]
    field_real = aperture * jnp.cos(angles)
    field_imag = aperture * jnp.sin(angles)
    half_real, half_imag = right_apply(field_real, field_imag, wide_real.T, wide_imag.T)
    spread_real, spread_imag = left_apply(wide_real, wide_imag, half_real, half_imag)
    psf_now = (spread_real * spread_real + spread_imag * spread_imag) / psf_norm
    quarter_real = contract("cfxy,yv->cfxv", psf_now, full_real)
    quarter_imag = contract("cfxy,yv->cfxv", psf_now, full_imag)
    otf_real, otf_imag = left_apply(full_real, full_imag, quarter_real, quarter_imag)
    object_real = gathered[:, 0][:, None]
    object_imag = gathered[:, 1][:, None]
    resid_real = object_real * otf_real - object_imag * otf_imag - images[:, :, 0]
    resid_imag = object_real * otf_imag + object_imag * otf_real - images[:, :, 1]
    object_term = jnp.stack(
        [
            jnp.sum(otf_real * resid_real + otf_imag * resid_imag, axis=1),
            jnp.sum(otf_real * resid_imag - otf_imag * resid_real, axis=1),
        ],
        axis=1,
    )
    obj_grad = lax.psum_scatter(object_term, "frame", scatter_dimension=2, tiled=True)
    weight_real = object_real * resid_real + object_imag * resid_imag
    weight_imag = object_real * resid_imag - object_imag * resid_real
    step_real, step_imag = right_apply(weight_real, weight_imag, full_real, -full_imag)
    along_psf = contract("ux,cfxv->cfuv", full_real, step_real) + contract(
        "ux,cfxv->cfuv", full_imag, step_imag
    )
    along_real = 2.0 / psf_norm * along_psf * spread_real
    along_imag = 2.0 / psf_norm * along_psf * spread_imag
    back_real, back_imag = right_apply(along_real, along_imag, wide_real, -wide_imag)
    grad_real, grad_imag = left_apply(wide_real.T, -wide_imag.T, back_real, back_imag)
    along_angle = field_real * grad_imag - field_imag * grad_real
    phase_grad = jnp.sum(phase_scale[:, None, None, None] * along_angle, axis=0)
    mode_grad = lax.psum(contract("fxy,mxy->fm", phase_grad, full_maps), "chan")
    return (obj_grad, mode_grad)


def solution(mesh):
    return jax.shard_map(
        on_device,
        mesh=mesh,
        in_specs=(
            P("chan", "frame", None, None, None),
            P("chan", None, "frame", None),
            P("frame", None),
            P(None, "chan", None),
            P(),
            P("chan"),
        ),
        out_specs=(P("chan", None, "frame", None), P("frame", None)),
        check_vma=False,
    )
```

profile of v0, /device:TPU:1, one launch (start us, length us, event | category | flops | bytes accessed | tf_op | source)
XLA Modules:
  0.0 503.8 jit_solution(15945762966751741058)
XLA Ops:
  7.2 0.0 copy-start
  7.2 0.0 all-gather.5.cloned.1.call-start
  7.2 1.5 copy.41
  8.7 0.0 all-gather.5.cloned.1.call-update
  8.8 0.0 all-gather.3.cloned.1.call-start
  8.8 0.7 all-gather.3.cloned.1.call-update
  9.5 0.0 all-reduce.3.cloned.1.call-start
  9.6 1.8 fusion.275
  11.3 0.0 copy-start.8
  11.4 0.3 copy.81
  11.7 1.4 copy.82
  13.1 0.7 multiply_reduce_fusion
  13.7 0.1 copy.49
  14.5 1.3 dynamic-slice
  16.5 60.8 %all-gather.5.cloned.1.call-done = f32[4,2,256,256]{3,0,1,2:T(4,128)} async-done(((f32[4,2,8,256]{3,0,1,2:T(4,128)}), f32[4,2,256,256]{3,0,1,2:T(4,128)}) %all-gather.5.cloned.1.call-update) | async-done | bytes 2097168 | tf_op jit(solution)/shard_map/all_gather | solution.py:54
  77.2 2.9 fusion.276
  80.1 1.6 copy.79
  81.7 0.0 copy-start.9
  81.7 1.4 copy.80
  83.0 60.2 %all-gather.3.cloned.1.call-done = f32[36,128,128]{2,1,0:T(8,128)} async-done(((f32[36,8,128]{2,1,0:T(8,128)}), f32[36,128,128]{2,1,0:T(8,128)}) %all-gather.3.cloned.1.call-update) | async-done | bytes 2359312 | tf_op jit(solution)/shard_map/all_gather | solution.py:52
  143.2 0.0 copy-done
  143.3 4.3 fusion.2
  147.6 1.8 fusion.40
  149.4 1.8 fusion.38
  151.3 1.8 convolution_subtract_fusion.4
  153.1 1.9 fusion.82
  155.1 1.5 fusion.94
  156.6 1.8 convolution_add_fusion.5
  158.4 1.5 convolution_add_fusion
  159.9 1.5 convolution_subtract_fusion
  161.4 2.2 fusion.31
  163.6 0.0 copy-done.5
  163.6 2.2 fusion.29
  165.8 2.1 fusion.62
  167.9 2.0 fusion.53
  170.0 2.0 fusion.6
  172.0 2.4 multiply_subtract_fusion
  174.4 0.5 multiply_add_fusion
  174.9 2.1 fusion.25
  177.0 2.3 fusion.27
  179.3 3.1 convolution_add_fusion.2
  182.3 2.1 convolution_subtract_fusion.1
  184.4 3.0 fusion.58
  187.4 1.5 pad_maximum_fusion
  188.9 3.4 copy.48
  192.4 0.0 all-reduce.3.cloned.1.call-update
  192.4 3.6 fusion.4
  196.0 3.0 fusion.21
  199.1 0.1 copy.60
  199.2 3.3 convolution_subtract_fusion.3
  202.4 0.0 copy-start.3
  202.4 1.3 fusion.87
  203.8 1.3 fusion.100
  205.2 2.2 fusion.19
  207.4 0.0 copy-done.3
  207.4 2.4 convolution_add_fusion.4
  209.8 2.1 fusion.8
  211.9 2.2 fusion.13
  214.1 0.1 copy.77
  214.2 3.0 fusion.14
  217.2 29.5 %psum.7 = f32[1,36]{1,0:T(1,128)} all-reduce(f32[1,36]{1,0:T(1,128)S(1)} %fusion.14), channel_id=1, replica_groups=mesh['chan'=16,'frame'=32] {'chan'}, use_global_device_ids=true, to_apply=%region_3.4 | all-reduce | flops 36 | bytes 288 | tf_op jit(solution)/shard_map/psum | solution.py:90
  246.7 248.9 %all-reduce.3.cloned.1.call-done = f32[4,2,256,256]{3,0,1,2:T(4,128)} async-done(((f32[4,2,256,256]{3,0,1,2:T(4,128)}), f32[4,2,256,256]{3,0,1,2:T(4,128)}) %all-reduce.3.cloned.1.call-update) | async-done | bytes 2097168
  495.6 0.8 constant_dynamic-slice_fusion
  496.4 0.7 copy.58
  (14 shorter events, 0.0 us)
Async XLA Ops:
  7.2 136.1 %copy-start = (f32[1,36]{1,0:T(1,128)S(1)}, f32[1,36]{1,0:T(1,128)}, u32[]{:S(2)}) copy-start(f32[1,36]{1,0:T(1,128)} %param.8) | copy-start | bytes 436
  7.2 70.0 %all-gather.5.cloned.1.call-start = ((), (), s32[]{:S(2)}) async-start(), calls=%async_computation.1 | async-start | bytes 2162688 | tf_op jit(solution)/shard_map/all_gather | solution.py:54
  8.8 134.5 %all-gather.3.cloned.1.call-start = ((), (), s32[]{:S(2)}) async-start(), calls=%async_computation | async-start | bytes 2506752 | tf_op jit(solution)/shard_map/all_gather | solution.py:52
  9.5 486.0 %all-reduce.3.cloned.1.call-start = ((), (), s32[]{:S(2)}) async-start(), calls=%async_computation.2 | async-start | bytes 4194304
  11.3 1.7 copy-start.8
  81.7 65.9 %copy-start.9 = (f32[4]{0:T(128)S(1)}, f32[4]{0:T(128)}, u32[]{:S(2)}) copy-start(f32[4]{0:T(128)} %param.11) | copy-start | bytes 52
  159.9 39.3 %copy-start.2 = (f32[4,256,256]{2,1,0:T(8,128)}, f32[4,256,256]{2,1,0:T(8,128)S(1)}, u32[]{:S(2)}) copy-start(f32[4,256,256]{2,1,0:T(8,128)S(1)} %convolution_add_fusion) | copy-start | bytes 3145732
  161.4 2.2 copy-start.5
  169.9 2.0 copy-start.4
  170.0 2.0 copy-start.7
  192.4 3.6 copy-start.6
  202.4 4.9 copy-start.3
  207.4 6.8 %copy-start.1 = (f32[36,128,128]{2,1,0:T(8,128)S(1)}, f32[36,128,128]{2,1,0:T(8,128)}, u32[]{:S(2)}) copy-start(f32[36,128,128]{2,1,0:T(8,128)} %all-gather.3.cloned.1.call-done) | copy-start | bytes 7077892
Sparse Core Ops, SparseCore 0:
  11.7 65.4 all-gather.4
  79.2 63.9 all-gather.2
  192.5 303.0 all-reduce.2
where the time goes:
time: 513 us; the launch traced here: 504 us
  waiting for transfers between devices  371 us (72%)
  matrix products  68 us (13%)
  blocking collectives  29.5 us (6%)
  local copies, waits for them, and re-layouts  17.3 us (3%)
  between operations  15.7 us (3%)
    unnamed x4, waiting for transfers between devices  250 us
    dot_general x30, matrix products, contract(): jnp.einsum(pattern, left_side, right_side, precision=HIGHEST, preferred_e...  68 us
    all_gather x1, waiting for transfers between devices, on_device(): gathered = lax.all_gather(objects, 'frame', axis=2, tiled=True)  60.8 us
    all_gather x1, waiting for transfers between devices, on_device(): full_maps = lax.all_gather(mode_maps, 'chan', axis=1, tiled=True)  60.2 us
    psum x1, blocking collectives, on_device(): mode_grad = lax.psum(contract('fxy,mxy->fm', phase_grad, full_maps), 'chan')  29.5 us
  transfers between devices with their start and end apart: 3, of which 3 were waited for; matrix products, arithmetic and copies ran while one was open for 7% of the time, Pallas kernels for 0%

commit v1 on v0

v1 whole, which is shorter than its diff:
```python
import functools
import math

import jax
import jax.numpy as jnp
import ml_dtypes
import numpy as np
from jax import lax
from jax.experimental import pallas as pl
from jax.experimental.pallas import tpu as pltpu
from jax.sharding import PartitionSpec as P

F32 = jnp.float32
BF16 = jnp.bfloat16
MESH = pl.DeviceIdType.MESH
GRID = 256
PUPIL = 128
SECT = 2304

T_A, T_B, T_L2, T_H, T_C, T_S, T_HT, T_BACK = 0, 256, 512, 768, 1024, 1280, 1536, 1792


def build_tables():
    index = np.arange(GRID)
    turn = (np.outer(index, index) % GRID) * (2.0 * math.pi / GRID)
    cos, sin = np.cos(turn), np.sin(turn)
    half = PUPIL
    first = np.concatenate([cos[:half], sin[:half]], 0)
    second = np.concatenate([-sin[:half], cos[:half]], 0)
    left = np.concatenate([cos[:, :half], sin[:, :half]], 1)
    minus = -sin[:, :half]
    minus[:, 0] = cos[:, half]
    herm = np.concatenate([cos[:, :half], minus], 1)
    back = np.concatenate(
        [
            np.concatenate([cos[:, :half], sin[:, :half]], 1),
            np.concatenate([-sin[:, :half], cos[:, :half]], 1),
        ],
        0,
    )
    table = np.concatenate([first, second, left, herm, cos, sin, herm.T, back], 0).astype(np.float32)
    high = table.astype(ml_dtypes.bfloat16)
    high = high.astype(np.float32)
    low = (table - high).astype(ml_dtypes.bfloat16).astype(np.float32)
    return np.concatenate([high, low], 0)


def split(value):
    high = value.astype(BF16)
    low = (value - high.astype(F32)).astype(BF16)
    return high, low


def dot(a, b):
    return jnp.dot(a, b, preferred_element_type=F32)


def dot3(a_high, a_low, b_high, b_low):
    left = jnp.concatenate([a_high, a_low, a_high], 1)
    right = jnp.concatenate([b_high, b_high, b_low], 0)
    return dot(left, right)


def sincos(angle):
    k = jnp.floor(angle * (2.0 / math.pi) + 0.5)
    r = ((angle - k * 1.5703125) - k * 4.837512969970703125e-4) - k * 7.54978995489188216e-8
    z = r * r
    sin_r = ((-1.9515295891e-4 * z + 8.3321608736e-3) * z - 1.6666654611e-1) * z * r + r
    cos_r = ((2.443315711809948e-5 * z - 1.388731625493765e-3) * z + 4.166664568298827e-2) * z * z - 0.5 * z + 1.0
    quad = k - 4.0 * jnp.floor(k * 0.25)
    odd = (quad == 1.0) | (quad == 3.0)
    sin_v = jnp.where(odd, cos_r, sin_r)
    cos_v = jnp.where(odd, sin_r, cos_r)
    sin_v = jnp.where(quad >= 2.0, -sin_v, sin_v)
    cos_v = jnp.where((quad == 1.0) | (quad == 2.0), -cos_v, cos_v)
    return sin_v, cos_v


def mirror(value):
    lane = lax.broadcasted_iota(jnp.int32, value.shape, 1)
    index = (PUPIL - lane) & (PUPIL - 1)
    return jnp.take_along_axis(value, index, axis=1, mode="promise_in_bounds")


def kernel(
    n_chan,
    channels,
    modes,
    images_hbm,
    objects_hbm,
    coeffs_hbm,
    maps_hbm,
    amp_hbm,
    scale_hbm,
    table_hbm,
    grad_ref,
    mode_ref,
    coeffs,
    scale,
    maps,
    amp,
    img,
    tab,
    obj,
    term,
    land_a,
    land_b1,
    land_b2,
    land_c1,
    land_c2,
    phases,
    field,
    pupil,
    half,
    spread,
    otf,
    weight,
    along,
    pgrad,
    land_pg,
    part,
    vec,
    land_vec,
    local_sem,
    peer_send,
    peer_recv,
    g_send,
    g_recv,
    r_send,
    r_recv,
):
    pairs = channels // 2
    me = lax.axis_index("chan")
    fr = lax.axis_index("frame")
    cx = lax.div(fr, 8)
    cy = lax.rem(lax.div(fr, 2), 4)
    cc = lax.rem(fr, 2)
    x_r, x_l = lax.rem(cx + 1, 4), lax.rem(cx + 3, 4)
    y_r, y_l = lax.rem(cy + 1, 4), lax.rem(cy + 3, 4)
    sib = 1 - cc
    dev_xr = x_r * 8 + cy * 2 + cc
    dev_xl = x_l * 8 + cy * 2 + cc
    dev_yr = cx * 8 + y_r * 2 + cc
    dev_yl = cx * 8 + y_l * 2 + cc
    dev_sib = cx * 8 + cy * 2 + sib
    core_at = cc * 16
    sib_at = sib * 16

    class Order:
        def __init__(self, major, minor, devices):
            self.col, self.col_r, self.col_l, self.col_o = [
                core_at + lax.rem(major + step, 4) * 4 for step in (0, 1, 3, 2)
            ]
            self.own, self.own_r, self.own_l, self.own_o = [
                self.col + lax.rem(minor + step, 4) for step in (0, 1, 3, 2)
            ]
            self.major_r, self.major_l, self.minor_r, self.minor_l = devices

    by_column = Order(cx, cy, (dev_xr, dev_xl, dev_yr, dev_yl))
    by_row = Order(cy, cx, (dev_yr, dev_yl, dev_xr, dev_xl))
    last = channels - 1

    def order(j):
        return by_row if j == last else by_column

    def peer(step):
        return lax.rem(me + step, n_chan)

    def local(k, src, dst):
        copy = pltpu.make_async_copy(src, dst, local_sem.at[k])
        copy.start()
        return copy

    maps_copy = local(0, maps_hbm, maps)
    coeffs_copy = local(1, coeffs_hbm, coeffs)
    obj_copies = [
        local(2, objects_hbm.at[pl.ds(0, last)], obj.at[pl.ds(0, last), by_column.own]),
        local(7, objects_hbm.at[last], obj.at[last, by_row.own]),
    ]
    scale_copy = local(3, scale_hbm, scale)
    amp_copy = local(4, amp_hbm, amp)
    tab_copy = local(5, table_hbm, tab)
    img_copy = local(6, images_hbm, img)
    barrier = pltpu.get_barrier_semaphore()
    for dev in (dev_yr, dev_yl, dev_xr, dev_xl, dev_sib):
        pl.semaphore_signal(barrier, inc=1, device_id={"frame": dev}, device_id_type=MESH)
    for step in range(1, n_chan):
        pl.semaphore_signal(barrier, inc=1, device_id={"chan": peer(step)}, device_id_type=MESH)

    maps_copy.wait()
    coeffs_copy.wait()
    mine = coeffs[0, 0] * maps[0]
    for m in range(1, modes):
        mine = mine + coeffs[0, m] * maps[m]
    phases[me] = mine
    for copy in obj_copies:
        copy.wait()
    pl.semaphore_wait(barrier, 5 + n_chan - 1)

    def frame_copy(src, dst, send, recv, dev):
        return pltpu.make_async_remote_copy(
            src_ref=src,
            dst_ref=dst,
            send_sem=send,
            recv_sem=recv,
            device_id={"frame": dev},
            device_id_type=MESH,
        )

    def chan_copy(src, dst, phase, dev):
        return pltpu.make_async_remote_copy(
            src_ref=src,
            dst_ref=dst,
            send_sem=peer_send.at[phase],
            recv_sem=peer_recv.at[phase],
            device_id={"chan": dev},
            device_id_type=MESH,
        )

    def gather_start(j, stage):
        o = order(j)
        across = []
        if stage == 0:
            sent = [(obj.at[j, o.own], o.minor_r), (obj.at[j, o.own], o.minor_l)]
        elif stage == 1:
            sent = [(obj.at[j, o.own_l, 0], o.minor_r), (obj.at[j, o.own_r, 1], o.minor_l)]
        elif stage == 2:
            sent = [(obj.at[j, pl.ds(o.col, 4)], o.major_r), (obj.at[j, pl.ds(o.col, 4)], o.major_l)]
            across = [o.col]
        elif stage == 3:
            sent = [
                (obj.at[j, pl.ds(o.col_l, 2)], o.major_r),
                (obj.at[j, pl.ds(o.col_r + 2, 2)], o.major_l),
            ]
            across = [o.col_r, o.col_l]
        else:
            sent = []
            across = [o.col_o]
        for src, dev in sent:
            frame_copy(src, src, g_send.at[j], g_recv.at[j, stage], dev).start()
        for col in across:
            src = obj.at[j, pl.ds(col, 4)]
            frame_copy(src, src, g_send.at[j], g_recv.at[j, 4], dev_sib).start()

    def gather_wait(j, stage):
        blocks = obj.at[j, pl.ds(0, (2, 1, 8, 4, 16)[stage])]
        frame_copy(blocks, blocks, g_send.at[j], g_recv.at[j, stage], dev_sib).wait_recv()

    def gather_next(j, stage):
        gather_wait(j, stage)
        gather_start(j, stage + 1)

    groups = ((0, 2), (2, 1), (3, 1))

    def reduce_start(g, stage):
        first, count = groups[g]
        o = order(first)
        here = pl.ds(first, count)
        if stage == 0:
            sent = [
                (term.at[here, pl.ds(sib_at + col, 4)], land_a.at[here, pl.ds(col, 4)], dev_sib)
                for col in [at - core_at for at in (o.col_o, o.col_r, o.col_l, o.col)]
            ]
        elif stage == 1:
            sent = [
                (term.at[here, pl.ds(o.col_o, 2)], land_b1.at[0, here], o.major_r),
                (term.at[here, pl.ds(o.col_o + 2, 2)], land_b1.at[1, here], o.major_l),
            ]
        elif stage == 2:
            sent = [
                (term.at[here, pl.ds(o.col_r, 4)], land_b2.at[0, here], o.major_r),
                (term.at[here, pl.ds(o.col_l, 4)], land_b2.at[1, here], o.major_l),
            ]
        elif stage == 3:
            sent = [
                (term.at[here, o.own_o, 0], land_c1.at[0, here], o.minor_r),
                (term.at[here, o.own_o, 1], land_c1.at[1, here], o.minor_l),
            ]
        else:
            sent = [
                (term.at[here, o.own_r], land_c2.at[0, here], o.minor_r),
                (term.at[here, o.own_l], land_c2.at[1, here], o.minor_l),
            ]
        for src, land, dev in sent:
            frame_copy(src, land, r_send.at[g], r_recv.at[g, stage], dev).start()

    def reduce_finish(g, stage):
        first, count = groups[g]
        o = order(first)
        here = pl.ds(first, count)
        blocks = term.at[here, pl.ds(0, (16, 4, 8, 1, 2)[stage])]
        frame_copy(blocks, blocks, r_send.at[g], r_recv.at[g, stage], dev_sib).wait_recv()
        for j in range(first, first + count):
            if stage == 0:
                at = pl.ds(core_at, 16)
                term[j, at] = term[j, at] + land_a[j]
            elif stage == 1:
                there, other = pl.ds(o.col_r, 2), pl.ds(o.col_l + 2, 2)
                term[j, there] = term[j, there] + land_b1[0, j]
                term[j, other] = term[j, other] + land_b1[1, j]
            elif stage == 2:
                at = pl.ds(o.col, 4)
                term[j, at] = term[j, at] + (land_b2[0, j] + land_b2[1, j])
            elif stage == 3:
                term[j, o.own_r, 0] = term[j, o.own_r, 0] + land_c1[0, j]
                term[j, o.own_l, 1] = term[j, o.own_l, 1] + land_c1[1, j]
            else:
                grad_ref[j] = term[j, o.own] + (land_c2[0, j] + land_c2[1, j])

    def reduce_next(g, stage):
        reduce_finish(g, stage)
        reduce_start(g, stage + 1)

    def each_peer(body):
        def run(step, carry):
            body(step)
            return carry

        lax.fori_loop(1, n_chan, run, 0)

    def peers_wait(phase, blocks, sent):
        copy = chan_copy(blocks, blocks, phase, peer(1))
        if sent:
            copy.wait_send()
        else:
            copy.wait_recv()

    others = pl.ds(0, n_chan - 1)
    each_peer(lambda step: chan_copy(phases.at[me], phases.at[me], 0, peer(step)).start())
    sequence = (3, 0, 1, 2)
    for j in sequence:
        gather_start(j, 0)

    amp_copy.wait()
    scale_copy.wait()
    line = lax.broadcasted_iota(jnp.int32, (PUPIL, PUPIL), 0).astype(F32) - (PUPIL - 1) / 2.0
    column = lax.broadcasted_iota(jnp.int32, (PUPIL, PUPIL), 1).astype(F32) - (PUPIL - 1) / 2.0
    inside = line * line + column * column <= (PUPIL / 2.0) ** 2
    aperture = jnp.where(inside, amp[...], 0.0)
    total = jnp.sum(aperture * aperture, axis=(0, 1), keepdims=True)
    inverse = 1.0 / (total * float(GRID * GRID))

    for stage in (0, 1):
        for j in sequence:
            gather_next(j, stage)
    peers_wait(0, phases.at[others], False)
    tab_copy.wait()

    def table(first, count=256):
        return (
            tab[pl.ds(first, count), :].astype(BF16),
            tab[pl.ds(SECT + first, count), :].astype(BF16),
        )

    wave = phases[...].reshape(PUPIL, PUPIL)

    def fields(j, carry):
        sin_v, cos_v = sincos(scale[j] * wave)
        real, imag = aperture * cos_v, aperture * sin_v
        field[j, 0] = real
        field[j, 1] = imag
        at = pl.ds(pl.multiple_of(j * PUPIL, PUPIL), PUPIL)
        pupil[at, pl.ds(0, PUPIL)] = real
        pupil[at, pl.ds(PUPIL, PUPIL)] = imag
        return carry

    lax.fori_loop(0, channels, fields, 0)
    x_hi, x_lo = split(pupil[...])
    half[:, 0:GRID] = dot3(x_hi, x_lo, *table(T_A))
    half[:, GRID : 2 * GRID] = dot3(x_hi, x_lo, *table(T_B))

    first_lane = lax.broadcasted_iota(jnp.int32, (GRID, PUPIL), 1) == 0

    def forward(p, carry):
        density = []
        for s in range(2):
            j = 2 * p + s
            at = pl.ds(pl.multiple_of(j * PUPIL, PUPIL), PUPIL)
            r_hi, r_lo = split(half[at, 0:GRID])
            i_hi, i_lo = split(half[at, GRID : 2 * GRID])
            high = jnp.concatenate(
                [jnp.concatenate([r_hi, i_hi], 1), jnp.concatenate([i_hi, -r_hi], 1)], 0
            )
            low = jnp.concatenate(
                [jnp.concatenate([r_lo, i_lo], 1), jnp.concatenate([i_lo, -r_lo], 1)], 0
            )
            both = dot3(*table(T_L2), high, low)
            spread[j] = both
            real, imag = both[:, 0:GRID], both[:, GRID : 2 * GRID]
            density.append((real * real + imag * imag) * inverse)
        q_hi, q_lo = split(dot3(*split(jnp.concatenate(density, 0)), *table(T_H)))

        @pl.when(p == 0)
        def _():
            gather_next(0, 2)
            gather_next(3, 2)

        @pl.when(p == 1)
        def _():
            gather_next(2, 2)
            gather_next(1, 3)

        for s in range(2):
            j = 2 * p + s
            at = slice(s * GRID, (s + 1) * GRID)
            product = dot3(*table(T_C, 512), q_hi[at], q_lo[at])
            by_cos, by_sin = product[0:GRID], product[GRID : 2 * GRID]
            p1, p3 = by_cos[:, 0:PUPIL], by_cos[:, PUPIL:GRID]
            p4, p2 = by_sin[:, 0:PUPIL], by_sin[:, PUPIL:GRID]
            otf[j, :, 0:PUPIL] = p1 + jnp.where(first_lane, 0.0, p2)
            otf[j, :, GRID : GRID + PUPIL] = jnp.where(first_lane, 0.0, p3) - p4
            otf[j, :, PUPIL:GRID] = mirror(jnp.where(first_lane, p3, p1 - p2))
            otf[j, :, GRID + PUPIL : 2 * GRID] = mirror(jnp.where(first_lane, -p2, -p3 - p4))

        @pl.when(p == 0)
        def _():
            gather_next(1, 2)
            gather_next(0, 3)

        @pl.when(p == 1)
        def _():
            gather_next(3, 3)
            gather_next(2, 3)

        return carry

    lax.fori_loop(0, pairs, forward, 0)
    img_copy.wait()

    lane0 = lax.broadcasted_iota(jnp.int32, (16, PUPIL), 1) == 0

    def residual_block(p, s, b):
        j = 2 * p + s
        at = pl.ds(pl.multiple_of(b * 16, 16), 16)
        at_low = pl.ds(pl.multiple_of(b * 16 + GRID, 16), 16)
        crossed = lax.rem(b, 4) * 4 + lax.div(b, 4)
        k = jnp.where(j == last, crossed, b) if s == 1 else b
        o_r = jnp.concatenate([obj[j, k, 0], obj[j, k + 16, 0]], 0)
        o_i = jnp.concatenate([obj[j, k, 1], obj[j, k + 16, 1]], 0)
        t_r, t_i = otf[j, at, 0:GRID], otf[j, at, GRID : 2 * GRID]
        r_r = o_r * t_r - o_i * t_i - img[j, 0, 0, at, :]
        r_i = o_r * t_i + o_i * t_r - img[j, 0, 1, at, :]
        g_r = t_r * r_r + t_i * r_i
        g_i = t_r * r_i - t_i * r_r
        term[j, k, 0] = g_r[0:8]
        term[j, k + 16, 0] = g_r[8:16]
        term[j, k, 1] = g_i[0:8]
        term[j, k + 16, 1] = g_i[8:16]
        w_r = o_r * r_r + o_i * r_i
        w_i = o_r * r_i - o_i * r_r
        wr_p, wi_p = w_r[:, 0:PUPIL], w_i[:, 0:PUPIL]
        wr_m, wi_m = mirror(w_r[:, PUPIL:GRID]), mirror(w_i[:, PUPIL:GRID])
        top = jnp.concatenate(
            [wr_p + jnp.where(lane0, 0.0, wr_m), jnp.where(lane0, wr_m, wi_p - wi_m)], 1
        )
        low = jnp.concatenate(
            [-(wi_p + jnp.where(lane0, 0.0, wi_m)), jnp.where(lane0, -wi_m, wr_p - wr_m)], 1
        )
        weight[j, at, :] = top
        weight[j, at_low, :] = low

    def residual(p):
        def run(b, carry):
            for s in range(2):
                residual_block(p, s, b)
            return carry

        lax.fori_loop(0, GRID // 16, run, 0, unroll=2)

    pgrad[...] = jnp.zeros_like(pgrad)

    def way_back(p, carry):
        gather_wait(2 * p, 4)
        gather_wait(2 * p + 1, 4)
        residual(p)

        @pl.when(p == 0)
        def _():
            reduce_start(0, 0)

        @pl.when(p == 1)
        def _():
            reduce_start(1, 0)
            reduce_start(2, 0)
            reduce_next(0, 1)

        c_hi, c_lo = table(T_C)
        s_hi, s_lo = table(T_S)
        high = jnp.concatenate([c_hi, s_hi], 1)
        low = jnp.concatenate([c_lo, s_lo], 1)
        back = jnp.concatenate([dot3(high, low, *split(weight[2 * p + s])) for s in range(2)], 0)
        change = dot3(*split(back), *table(T_HT)) * (2.0 * inverse)
        for s in range(2):
            j = 2 * p + s
            at = pl.ds(s * GRID, GRID)
            here = change[s * GRID : (s + 1) * GRID]
            for part_at in (pl.ds(0, GRID), pl.ds(GRID, GRID)):
                along[p, at, part_at] = here * spread[j, :, part_at]

        @pl.when(p == 0)
        def _():
            reduce_next(0, 0)

        @pl.when(p == 1)
        def _():
            reduce_next(1, 0)
            reduce_next(2, 0)

        return carry

    lax.fori_loop(0, pairs, way_back, 0)

    def to_pupil(p, carry):
        b_hi, b_lo = split(dot3(*split(along[p]), *table(T_BACK, 512)))
        for s in range(2):
            j = 2 * p + s
            at = slice(s * GRID, (s + 1) * GRID)
            g = dot3(*table(T_A), b_hi[at], b_lo[at])
            g_r = g[0:PUPIL, 0:PUPIL] - g[PUPIL:GRID, PUPIL:GRID]
            g_i = g[PUPIL:GRID, 0:PUPIL] + g[0:PUPIL, PUPIL:GRID]
            change = scale[j] * (field[j, 0] * g_i - field[j, 1] * g_r)
            pgrad[...] = pgrad[...] + change.reshape(pgrad.shape)

        @pl.when(p == 0)
        def _():
            reduce_next(1, 1)
            reduce_next(2, 1)
            reduce_next(0, 2)

        return carry

    lax.fori_loop(0, pairs, to_pupil, 0)
    each_peer(lambda step: chan_copy(pgrad.at[peer(step)], land_pg.at[step], 1, peer(step)).start())
    reduce_next(0, 3)
    reduce_next(1, 2)
    reduce_next(2, 2)

    part[...] = jnp.zeros_like(part)
    peers_wait(1, land_pg.at[others], False)
    summed = pgrad[me]
    for step in range(1, n_chan):
        summed = summed + land_pg[step]
    for m in range(modes):
        part[m : m + 1, :] = jnp.sum(maps[m] * summed, axis=0, keepdims=True)
    vec[...] = lax.dot_general(
        jnp.ones((8, PUPIL), F32),
        part[...],
        (((1,), (1,)), ((), ())),
        precision=lax.Precision.HIGHEST,
        preferred_element_type=F32,
    )
    each_peer(lambda step: chan_copy(vec, land_vec.at[step], 2, peer(step)).start())
    reduce_next(1, 3)
    reduce_next(2, 3)
    reduce_finish(0, 4)
    peers_wait(2, land_vec.at[others], False)
    answer = vec[...]
    for step in range(1, n_chan):
        answer = answer + land_vec[step]
    mode_ref[...] = answer[0:1, 0:modes]
    reduce_finish(1, 4)
    reduce_finish(2, 4)

    for j in range(channels):
        blocks = obj.at[j, pl.ds(0, 31)]
        frame_copy(blocks, blocks, g_send.at[j], g_recv.at[j, 0], dev_sib).wait_send()
    for g, (first, count) in enumerate(groups):
        blocks = term.at[pl.ds(first, count), pl.ds(0, 31)]
        frame_copy(blocks, blocks, r_send.at[g], r_recv.at[g, 0], dev_sib).wait_send()
    peers_wait(0, phases.at[others], True)
    peers_wait(1, land_pg.at[others], True)
    peers_wait(2, land_vec.at[others], True)


def on_device(n_chan, images, objects, coeffs, mode_maps, amplitude, phase_scale):
    channels = images.shape[0]
    modes = coeffs.shape[1]
    rows = mode_maps.shape[1]
    vmem = pl.BlockSpec(memory_space=pltpu.VMEM)
    hbm = pl.BlockSpec(memory_space=pltpu.HBM)
    dma = pltpu.SemaphoreType.DMA
    block = (2, 8, GRID)
    two = channels // 2
    outs = (
        jax.ShapeDtypeStruct(objects.shape, F32),
        jax.ShapeDtypeStruct(coeffs.shape, F32),
    )
    inputs = (images, objects, coeffs, mode_maps, amplitude, phase_scale, jnp.asarray(build_tables()))
    return pl.pallas_call(
        functools.partial(kernel, n_chan, channels, modes),
        out_shape=outs,
        in_specs=[hbm] * 7,
        out_specs=(vmem, vmem),
        scratch_shapes=[
            pltpu.SMEM(coeffs.shape, F32),
            pltpu.SMEM(phase_scale.shape, F32),
            pltpu.VMEM(mode_maps.shape, F32),
            pltpu.VMEM(amplitude.shape, F32),
            pltpu.VMEM(images.shape, F32),
            pltpu.VMEM((2 * SECT, GRID), F32),
            pltpu.VMEM((channels, 32) + block, F32),
            pltpu.VMEM((channels, 32) + block, F32),
            pltpu.VMEM((channels, 16) + block, F32),
            pltpu.VMEM((2, channels, 2) + block, F32),
            pltpu.VMEM((2, channels, 4) + block, F32),
            pltpu.VMEM((2, channels, 8, GRID), F32),
            pltpu.VMEM((2, channels) + block, F32),
            pltpu.VMEM((n_chan, rows, PUPIL), F32),
            pltpu.VMEM((channels, 2, PUPIL, PUPIL), F32),
            pltpu.VMEM((channels * PUPIL, GRID), F32),
            pltpu.VMEM((channels * PUPIL, 2 * GRID), F32),
            pltpu.VMEM((channels, GRID, 2 * GRID), F32),
            pltpu.VMEM((channels, GRID, 2 * GRID), F32),
            pltpu.VMEM((channels, 2 * GRID, GRID), F32),
            pltpu.VMEM((two, 2 * GRID, 2 * GRID), F32),
            pltpu.VMEM((n_chan, rows, PUPIL), F32),
            pltpu.VMEM((n_chan, rows, PUPIL), F32),
            pltpu.VMEM((PUPIL, PUPIL), F32),
            pltpu.VMEM((8, PUPIL), F32),
            pltpu.VMEM((n_chan, 8, PUPIL), F32),
            dma((8,)),
            dma((3,)),
            dma((3,)),
            dma((channels,)),
            dma((channels, 5)),
            dma((3,)),
            dma((3, 5)),
        ],
        compiler_params=pltpu.CompilerParams(
            collective_id=0, has_side_effects=True, vmem_limit_bytes=48 * 1024 * 1024
        ),
        name="deconvolve",
    )(*[pltpu.with_memory_space_constraint(value, pltpu.HBM) for value in inputs])


def solution(mesh):
    return jax.shard_map(
        functools.partial(on_device, mesh.shape["chan"]),
        mesh=mesh,
        in_specs=(
            P("chan", "frame", None, None, None),
            P("chan", None, "frame", None),
            P("frame", None),
            P(None, "chan", None),
            P(),
            P("chan"),
        ),
        out_specs=(P("chan", None, "frame", None), P("frame", None)),
        check_vma=False,
    )
```

time: 513 us -> 62.4 us (0.12)
  the two profiles are of different devices: /device:TPU:1 before, /device:TPU:24 now
where the time goes in v1:
time: 62.4 us; the launch traced here: 62.3 us
  Pallas kernels  60.5 us (97%)
  local copies, waits for them, and re-layouts  1.14 us (2%)
  between operations  0.64 us (1%)
    pallas_call x1, Pallas kernels, on_device(): pl.pallas_call(functools.partial(kernel, n_chan, channels, modes), out_sh...  60.5 us

profile of v1, /device:TPU:24, one launch (start us, length us, event | category | flops | bytes accessed | tf_op | source)
XLA Modules:
  0.0 62.3 jit_solution(16509000372732970907)
XLA Ops:
  0.6 60.5 %deconvolve.1 = (f32[4,2,8,256]{3,2,1,0:T(8,128)S(1)}, f32[1,36]{1,0:T(1,128)S(1)}) custom-call(f32[4,1,2,256,256]{4,3,2,1,0:T(8,128)} %images_hbm.1, f32[4,2,8,256]{3,2,1,0:T(8,128)} %objects_hbm.1, f32[1,36]{1,0:T(1,128)} %coeffs_hbm.1, f32[36,8,128]{2,1,0:T(8,128)} %maps_hbm.1, f32[128,128]{1,0:T(8,128)} %amp_hbm.1, f32[4]{0:T(128)} %scale_hbm.1, ...), custom_call_target="tpu_custom_call" | custom-call | tf_op jit(solution)/shard_map/deconvolve/pallas_call | solution.py:589
  61.1 0.6 %copy.11 = f32[4,2,8,256]{3,2,1,0:T(8,128)} copy(f32[4,2,8,256]{3,2,1,0:T(8,128)S(1)} %get-tuple-element.4) | data formatting | bytes 131072
  61.7 0.5 copy.12

commit v2 on v1

--- a/solution.py
+++ b/solution.py
@@ -142,6 +142,8 @@
     dev_xl = x_l * 8 + cy * 2 + cc
     dev_yr = cx * 8 + y_r * 2 + cc
     dev_yl = cx * 8 + y_l * 2 + cc
+    dev_xo = lax.rem(cx + 2, 4) * 8 + cy * 2 + cc
+    dev_yo = cx * 8 + lax.rem(cy + 2, 4) * 2 + cc
     dev_sib = cx * 8 + cy * 2 + sib
     core_at = cc * 16
     sib_at = sib * 16
@@ -154,10 +156,10 @@
             self.own, self.own_r, self.own_l, self.own_o = [
                 self.col + lax.rem(minor + step, 4) for step in (0, 1, 3, 2)
             ]
-            self.major_r, self.major_l, self.minor_r, self.minor_l = devices
-
-    by_column = Order(cx, cy, (dev_xr, dev_xl, dev_yr, dev_yl))
-    by_row = Order(cy, cx, (dev_yr, dev_yl, dev_xr, dev_xl))
+            self.major_r, self.major_l, self.minor_r, self.minor_l, self.minor_o = devices
+
+    by_column = Order(cx, cy, (dev_xr, dev_xl, dev_yr, dev_yl, dev_yo))
+    by_row = Order(cy, cx, (dev_yr, dev_yl, dev_xr, dev_xl, dev_xo))
     last = channels - 1
 
     def order(j):
@@ -182,7 +184,7 @@
     tab_copy = local(5, table_hbm, tab)
     img_copy = local(6, images_hbm, img)
     barrier = pltpu.get_barrier_semaphore()
-    for dev in (dev_yr, dev_yl, dev_xr, dev_xl, dev_sib):
+    for dev in (dev_yr, dev_yl, dev_yo, dev_xr, dev_xl, dev_xo, dev_sib):
         pl.semaphore_signal(barrier, inc=1, device_id={"frame": dev}, device_id_type=MESH)
     for step in range(1, n_chan):
         pl.semaphore_signal(barrier, inc=1, device_id={"chan": peer(step)}, device_id_type=MESH)
@@ -195,7 +197,7 @@
     phases[me] = mine
     for copy in obj_copies:
         copy.wait()
-    pl.semaphore_wait(barrier, 5 + n_chan - 1)
+    pl.semaphore_wait(barrier, 7 + n_chan - 1)
 
     def frame_copy(src, dst, send, recv, dev):
         return pltpu.make_async_remote_copy(
@@ -217,11 +219,16 @@
             device_id_type=MESH,
         )
 
+    at_once = (0,)
+    groups_at_once = (1, 2)
+
     def gather_start(j, stage):
         o = order(j)
         across = []
         if stage == 0:
             sent = [(obj.at[j, o.own], o.minor_r), (obj.at[j, o.own], o.minor_l)]
+            if j in at_once:
+                sent.append((obj.at[j, o.own], o.minor_o))
         elif stage == 1:
             sent = [(obj.at[j, o.own_l, 0], o.minor_r), (obj.at[j, o.own_r, 1], o.minor_l)]
         elif stage == 2:
@@ -243,12 +250,13 @@
             frame_copy(src, src, g_send.at[j], g_recv.at[j, 4], dev_sib).start()
 
     def gather_wait(j, stage):
-        blocks = obj.at[j, pl.ds(0, (2, 1, 8, 4, 16)[stage])]
+        direct = stage == 0 and not isinstance(j, jax.Array) and j in at_once
+        blocks = obj.at[j, pl.ds(0, 3 if direct else (2, 1, 8, 4, 16)[stage])]
         frame_copy(blocks, blocks, g_send.at[j], g_recv.at[j, stage], dev_sib).wait_recv()
 
     def gather_next(j, stage):
         gather_wait(j, stage)
-        gather_start(j, stage + 1)
+        gather_start(j, 2 if stage == 0 and j in at_once else stage + 1)
 
     groups = ((0, 2), (2, 1), (3, 1))
 
@@ -281,6 +289,8 @@
                 (term.at[here, o.own_r], land_c2.at[0, here], o.minor_r),
                 (term.at[here, o.own_l], land_c2.at[1, here], o.minor_l),
             ]
+            if g in groups_at_once:
+                sent.append((term.at[here, o.own_o], land_c2.at[2, here], o.minor_o))
         for src, land, dev in sent:
             frame_copy(src, land, r_send.at[g], r_recv.at[g, stage], dev).start()
 
@@ -288,7 +298,8 @@
         first, count = groups[g]
         o = order(first)
         here = pl.ds(first, count)
-        blocks = term.at[here, pl.ds(0, (16, 4, 8, 1, 2)[stage])]
+        direct = g in groups_at_once
+        blocks = term.at[here, pl.ds(0, (16, 4, 8, 1, 3 if direct else 2)[stage])]
         frame_copy(blocks, blocks, r_send.at[g], r_recv.at[g, stage], dev_sib).wait_recv()
         for j in range(first, first + count):
             if stage == 0:
@@ -305,11 +316,14 @@
                 term[j, o.own_r, 0] = term[j, o.own_r, 0] + land_c1[0, j]
                 term[j, o.own_l, 1] = term[j, o.own_l, 1] + land_c1[1, j]
             else:
-                grad_ref[j] = term[j, o.own] + (land_c2[0, j] + land_c2[1, j])
+                landed = land_c2[0, j] + land_c2[1, j]
+                if direct:
+                    landed = landed + land_c2[2, j]
+                grad_ref[j] = term[j, o.own] + landed
 
     def reduce_next(g, stage):
         reduce_finish(g, stage)
-        reduce_start(g, stage + 1)
+        reduce_start(g, 4 if stage == 2 and g in groups_at_once else stage + 1)
 
     def each_peer(body):
         def run(step, carry):
@@ -327,7 +341,7 @@
 
     others = pl.ds(0, n_chan - 1)
     each_peer(lambda step: chan_copy(phases.at[me], phases.at[me], 0, peer(step)).start())
-    sequence = (3, 0, 1, 2)
+    sequence = (0, 3, 1, 2)
     for j in sequence:
         gather_start(j, 0)
 
@@ -342,7 +356,8 @@
 
     for stage in (0, 1):
         for j in sequence:
-            gather_next(j, stage)
+            if not (stage == 1 and j in at_once):
+                gather_next(j, stage)
     peers_wait(0, phases.at[others], False)
     tab_copy.wait()
 
@@ -550,8 +565,6 @@
         preferred_element_type=F32,
     )
     each_peer(lambda step: chan_copy(vec, land_vec.at[step], 2, peer(step)).start())
-    reduce_next(1, 3)
-    reduce_next(2, 3)
     reduce_finish(0, 4)
     peers_wait(2, land_vec.at[others], False)
     answer = vec[...]
@@ -604,7 +617,7 @@
             pltpu.VMEM((2, channels, 2) + block, F32),
             pltpu.VMEM((2, channels, 4) + block, F32),
             pltpu.VMEM((2, channels, 8, GRID), F32),
-            pltpu.VMEM((2, channels) + block, F32),
+            pltpu.VMEM((3, channels) + block, F32),
             pltpu.VMEM((n_chan, rows, PUPIL), F32),
             pltpu.VMEM((channels, 2, PUPIL, PUPIL), F32),
             pltpu.VMEM((channels * PUPIL, GRID), F32),

time: 62.4 us -> 63 us (level)
  the two profiles are of different devices: /device:TPU:24 before, /device:TPU:1 now
where the time goes in v2:
time: 63 us; the launch traced here: 62.9 us
  Pallas kernels  61.1 us (97%)
  local copies, waits for them, and re-layouts  1.14 us (2%)
  between operations  0.64 us (1%)
    pallas_call x1, Pallas kernels, on_device(): pl.pallas_call(functools.partial(kernel, n_chan, channels, modes), out_sh...  61.1 us

profile of v2, /device:TPU:1, one launch (start us, length us, event | category | flops | bytes accessed | tf_op | source)
XLA Modules:
  0.0 62.9 jit_solution(14737374889635483443)
XLA Ops:
  0.6 61.1 %deconvolve.1 = (f32[4,2,8,256]{3,2,1,0:T(8,128)S(1)}, f32[1,36]{1,0:T(1,128)S(1)}) custom-call(f32[4,1,2,256,256]{4,3,2,1,0:T(8,128)} %images_hbm.1, f32[4,2,8,256]{3,2,1,0:T(8,128)} %objects_hbm.1, f32[1,36]{1,0:T(1,128)} %coeffs_hbm.1, f32[36,8,128]{2,1,0:T(8,128)} %maps_hbm.1, f32[128,128]{1,0:T(8,128)} %amp_hbm.1, f32[4]{0:T(128)} %scale_hbm.1, ...), custom_call_target="tpu_custom_call" | custom-call | tf_op jit(solution)/shard_map/deconvolve/pallas_call | solution.py:602
  61.7 0.6 %copy.11 = f32[4,2,8,256]{3,2,1,0:T(8,128)} copy(f32[4,2,8,256]{3,2,1,0:T(8,128)S(1)} %get-tuple-element.4) | data formatting | bytes 131072
  62.4 0.5 copy.12

commit v3 on v1

--- a/solution.py
+++ b/solution.py
@@ -15,9 +15,8 @@
 MESH = pl.DeviceIdType.MESH
 GRID = 256
 PUPIL = 128
-SECT = 2304
-
-T_A, T_B, T_L2, T_H, T_C, T_S, T_HT, T_BACK = 0, 256, 512, 768, 1024, 1280, 1536, 1792
+
+T_A, T_B, T_L2, T_H, T_C, T_S, T_HT, T_BACK = 0, 1, 2, 3, 4, 5, 6, 7
 
 
 def build_tables():
@@ -42,7 +41,7 @@
     high = table.astype(ml_dtypes.bfloat16)
     high = high.astype(np.float32)
     low = (table - high).astype(ml_dtypes.bfloat16).astype(np.float32)
-    return np.concatenate([high, low], 0)
+    return np.stack([high, low]).reshape(2, -1, GRID, GRID)
 
 
 def split(value):
@@ -109,13 +108,15 @@
     land_c1,
     land_c2,
     phases,
-    field,
     pupil,
     half,
     spread,
-    otf,
+    folded,
+    product,
     weight,
+    back,
     along,
+    last_rows,
     pgrad,
     land_pg,
     part,
@@ -346,85 +347,67 @@
     peers_wait(0, phases.at[others], False)
     tab_copy.wait()
 
-    def table(first, count=256):
-        return (
-            tab[pl.ds(first, count), :].astype(BF16),
-            tab[pl.ds(SECT + first, count), :].astype(BF16),
-        )
+    def table(k):
+        return tab[0, k].astype(BF16), tab[1, k].astype(BF16)
+
+    def each_channel(body):
+        def run(j, carry):
+            body(j)
+            return carry
+
+        lax.fori_loop(0, channels, run, 0)
+
+    def each_half(body):
+        def run(i, carry):
+            body(lax.div(i, 2), lax.rem(i, 2))
+            return carry
+
+        lax.fori_loop(0, 2 * channels, run, 0)
 
     wave = phases[...].reshape(PUPIL, PUPIL)
 
-    def fields(j, carry):
+    def fields(j):
         sin_v, cos_v = sincos(scale[j] * wave)
         real, imag = aperture * cos_v, aperture * sin_v
-        field[j, 0] = real
-        field[j, 1] = imag
-        at = pl.ds(pl.multiple_of(j * PUPIL, PUPIL), PUPIL)
-        pupil[at, pl.ds(0, PUPIL)] = real
-        pupil[at, pl.ds(PUPIL, PUPIL)] = imag
-        return carry
-
-    lax.fori_loop(0, channels, fields, 0)
-    x_hi, x_lo = split(pupil[...])
-    half[:, 0:GRID] = dot3(x_hi, x_lo, *table(T_A))
-    half[:, GRID : 2 * GRID] = dot3(x_hi, x_lo, *table(T_B))
-
-    first_lane = lax.broadcasted_iota(jnp.int32, (GRID, PUPIL), 1) == 0
-
-    def forward(p, carry):
-        density = []
-        for s in range(2):
-            j = 2 * p + s
-            at = pl.ds(pl.multiple_of(j * PUPIL, PUPIL), PUPIL)
-            r_hi, r_lo = split(half[at, 0:GRID])
-            i_hi, i_lo = split(half[at, GRID : 2 * GRID])
-            high = jnp.concatenate(
-                [jnp.concatenate([r_hi, i_hi], 1), jnp.concatenate([i_hi, -r_hi], 1)], 0
-            )
-            low = jnp.concatenate(
-                [jnp.concatenate([r_lo, i_lo], 1), jnp.concatenate([i_lo, -r_lo], 1)], 0
-            )
-            both = dot3(*table(T_L2), high, low)
-            spread[j] = both
-            real, imag = both[:, 0:GRID], both[:, GRID : 2 * GRID]
-            density.append((real * real + imag * imag) * inverse)
-        q_hi, q_lo = split(dot3(*split(jnp.concatenate(density, 0)), *table(T_H)))
-
-        @pl.when(p == 0)
-        def _():
-            gather_next(0, 2)
-            gather_next(3, 2)
-
-        @pl.when(p == 1)
-        def _():
-            gather_next(2, 2)
-            gather_next(1, 3)
-
-        for s in range(2):
-            j = 2 * p + s
-            at = slice(s * GRID, (s + 1) * GRID)
-            product = dot3(*table(T_C, 512), q_hi[at], q_lo[at])
-            by_cos, by_sin = product[0:GRID], product[GRID : 2 * GRID]
-            p1, p3 = by_cos[:, 0:PUPIL], by_cos[:, PUPIL:GRID]
-            p4, p2 = by_sin[:, 0:PUPIL], by_sin[:, PUPIL:GRID]
-            otf[j, :, 0:PUPIL] = p1 + jnp.where(first_lane, 0.0, p2)
-            otf[j, :, GRID : GRID + PUPIL] = jnp.where(first_lane, 0.0, p3) - p4
-            otf[j, :, PUPIL:GRID] = mirror(jnp.where(first_lane, p3, p1 - p2))
-            otf[j, :, GRID + PUPIL : 2 * GRID] = mirror(jnp.where(first_lane, -p2, -p3 - p4))
-
-        @pl.when(p == 0)
-        def _():
-            gather_next(1, 2)
-            gather_next(0, 3)
-
-        @pl.when(p == 1)
-        def _():
-            gather_next(3, 3)
-            gather_next(2, 3)
-
-        return carry
-
-    lax.fori_loop(0, pairs, forward, 0)
+        pupil[j, :, 0:PUPIL] = real
+        pupil[j, :, PUPIL:GRID] = imag
+
+    each_channel(fields)
+
+    def pupil_rows(j):
+        x_hi, x_lo = split(pupil[j])
+        real = dot3(x_hi, x_lo, *table(T_A))
+        imag = dot3(x_hi, x_lo, *table(T_B))
+        half[j, 0, 0:PUPIL, :] = real
+        half[j, 0, PUPIL:GRID, :] = imag
+        half[j, 1, 0:PUPIL, :] = imag
+        half[j, 1, PUPIL:GRID, :] = -real
+
+    each_channel(pupil_rows)
+    gather_next(0, 2)
+    gather_next(3, 2)
+
+    def to_spread(j, n):
+        spread[j, n] = dot3(*table(T_L2), *split(half[j, n]))
+
+    each_half(to_spread)
+    gather_next(1, 2)
+    gather_next(0, 3)
+
+    def fold(j):
+        real, imag = spread[j, 0], spread[j, 1]
+        folded[j] = dot3(*split((real * real + imag * imag) * inverse), *table(T_H))
+
+    each_channel(fold)
+    gather_next(2, 2)
+    gather_next(1, 3)
+
+    def products(j, t):
+        product[j, t] = dot3(*table(T_C + t), *split(folded[j]))
+
+    each_half(products)
+    gather_next(3, 3)
+    gather_next(2, 3)
     img_copy.wait()
 
     lane0 = lax.broadcasted_iota(jnp.int32, (16, PUPIL), 1) == 0
@@ -432,12 +415,18 @@
     def residual_block(p, s, b):
         j = 2 * p + s
         at = pl.ds(pl.multiple_of(b * 16, 16), 16)
-        at_low = pl.ds(pl.multiple_of(b * 16 + GRID, 16), 16)
         crossed = lax.rem(b, 4) * 4 + lax.div(b, 4)
         k = jnp.where(j == last, crossed, b) if s == 1 else b
         o_r = jnp.concatenate([obj[j, k, 0], obj[j, k + 16, 0]], 0)
         o_i = jnp.concatenate([obj[j, k, 1], obj[j, k + 16, 1]], 0)
-        t_r, t_i = otf[j, at, 0:GRID], otf[j, at, GRID : 2 * GRID]
+        p1, p3 = product[j, 0, at, 0:PUPIL], product[j, 0, at, PUPIL:GRID]
+        p4, p2 = product[j, 1, at, 0:PUPIL], product[j, 1, at, PUPIL:GRID]
+        t_r = jnp.concatenate(
+            [p1 + jnp.where(lane0, 0.0, p2), mirror(jnp.where(lane0, p3, p1 - p2))], 1
+        )
+        t_i = jnp.concatenate(
+            [jnp.where(lane0, 0.0, p3) - p4, mirror(jnp.where(lane0, -p2, -p3 - p4))], 1
+        )
         r_r = o_r * t_r - o_i * t_i - img[j, 0, 0, at, :]
         r_i = o_r * t_i + o_i * t_r - img[j, 0, 1, at, :]
         g_r = t_r * r_r + t_i * r_i
@@ -456,8 +445,8 @@
         low = jnp.concatenate(
             [-(wi_p + jnp.where(lane0, 0.0, wi_m)), jnp.where(lane0, -wi_m, wr_p - wr_m)], 1
         )
-        weight[j, at, :] = top
-        weight[j, at_low, :] = low
+        weight[j, 0, at, :] = top
+        weight[j, 1, at, :] = low
 
     def residual(p):
         def run(b, carry):
@@ -467,9 +456,7 @@
 
         lax.fori_loop(0, GRID // 16, run, 0, unroll=2)
 
-    pgrad[...] = jnp.zeros_like(pgrad)
-
-    def way_back(p, carry):
+    def pair_residual(p, carry):
         gather_wait(2 * p, 4)
         gather_wait(2 * p + 1, 4)
         residual(p)
@@ -482,54 +469,44 @@
         def _():
             reduce_start(1, 0)
             reduce_start(2, 0)
-            reduce_next(0, 1)
-
-        c_hi, c_lo = table(T_C)
-        s_hi, s_lo = table(T_S)
-        high = jnp.concatenate([c_hi, s_hi], 1)
-        low = jnp.concatenate([c_lo, s_lo], 1)
-        back = jnp.concatenate([dot3(high, low, *split(weight[2 * p + s])) for s in range(2)], 0)
-        change = dot3(*split(back), *table(T_HT)) * (2.0 * inverse)
-        for s in range(2):
-            j = 2 * p + s
-            at = pl.ds(s * GRID, GRID)
-            here = change[s * GRID : (s + 1) * GRID]
-            for part_at in (pl.ds(0, GRID), pl.ds(GRID, GRID)):
-                along[p, at, part_at] = here * spread[j, :, part_at]
-
-        @pl.when(p == 0)
-        def _():
-            reduce_next(0, 0)
-
-        @pl.when(p == 1)
-        def _():
-            reduce_next(1, 0)
-            reduce_next(2, 0)
 
         return carry
 
-    lax.fori_loop(0, pairs, way_back, 0)
-
-    def to_pupil(p, carry):
-        b_hi, b_lo = split(dot3(*split(along[p]), *table(T_BACK, 512)))
-        for s in range(2):
-            j = 2 * p + s
-            at = slice(s * GRID, (s + 1) * GRID)
-            g = dot3(*table(T_A), b_hi[at], b_lo[at])
-            g_r = g[0:PUPIL, 0:PUPIL] - g[PUPIL:GRID, PUPIL:GRID]
-            g_i = g[PUPIL:GRID, 0:PUPIL] + g[0:PUPIL, PUPIL:GRID]
-            change = scale[j] * (field[j, 0] * g_i - field[j, 1] * g_r)
-            pgrad[...] = pgrad[...] + change.reshape(pgrad.shape)
-
-        @pl.when(p == 0)
-        def _():
-            reduce_next(1, 1)
-            reduce_next(2, 1)
-            reduce_next(0, 2)
-
-        return carry
-
-    lax.fori_loop(0, pairs, to_pupil, 0)
+    lax.fori_loop(0, pairs, pair_residual, 0)
+
+    def unproducts(j, t):
+        back[j, t] = dot3(*table(T_C + t), *split(weight[j, t]))
+
+    each_half(unproducts)
+    reduce_next(0, 0)
+
+    def unfold(j):
+        change = dot3(*split(back[j, 0] + back[j, 1]), *table(T_HT)) * (2.0 * inverse)
+        along[j, 0] = change * spread[j, 0]
+        along[j, 1] = change * spread[j, 1]
+
+    each_channel(unfold)
+    reduce_next(1, 0)
+    reduce_next(2, 0)
+    reduce_next(0, 1)
+
+    def from_spread(j, n):
+        last_rows[j, n] = dot3(*split(along[j, n]), *table(T_BACK + n))
+
+    each_half(from_spread)
+    reduce_next(1, 1)
+    reduce_next(2, 1)
+    reduce_next(0, 2)
+    pgrad[...] = jnp.zeros_like(pgrad)
+
+    def to_pupil(j):
+        g = dot3(*table(T_A), *split(last_rows[j, 0] + last_rows[j, 1]))
+        g_r = g[0:PUPIL, 0:PUPIL] - g[PUPIL:GRID, PUPIL:GRID]
+        g_i = g[PUPIL:GRID, 0:PUPIL] + g[0:PUPIL, PUPIL:GRID]
+        change = scale[j] * (pupil[j, :, 0:PUPIL] * g_i - pupil[j, :, PUPIL:GRID] * g_r)
+        pgrad[...] = pgrad[...] + change.reshape(pgrad.shape)
+
+    each_channel(to_pupil)
     each_peer(lambda step: chan_copy(pgrad.at[peer(step)], land_pg.at[step], 1, peer(step)).start())
     reduce_next(0, 3)
     reduce_next(1, 2)
@@ -580,7 +557,6 @@
     hbm = pl.BlockSpec(memory_space=pltpu.HBM)
     dma = pltpu.SemaphoreType.DMA
     block = (2, 8, GRID)
-    two = channels // 2
     outs = (
         jax.ShapeDtypeStruct(objects.shape, F32),
         jax.ShapeDtypeStruct(coeffs.shape, F32),
@@ -597,7 +573,7 @@
             pltpu.VMEM(mode_maps.shape, F32),
             pltpu.VMEM(amplitude.shape, F32),
             pltpu.VMEM(images.shape, F32),
-            pltpu.VMEM((2 * SECT, GRID), F32),
+            pltpu.VMEM((2, 9, GRID, GRID), F32),
             pltpu.VMEM((channels, 32) + block, F32),
             pltpu.VMEM((channels, 32) + block, F32),
             pltpu.VMEM((channels, 16) + block, F32),
@@ -606,13 +582,15 @@
             pltpu.VMEM((2, channels, 8, GRID), F32),
             pltpu.VMEM((2, channels) + block, F32),
             pltpu.VMEM((n_chan, rows, PUPIL), F32),
-            pltpu.VMEM((channels, 2, PUPIL, PUPIL), F32),
-            pltpu.VMEM((channels * PUPIL, GRID), F32),
-            pltpu.VMEM((channels * PUPIL, 2 * GRID), F32),
-            pltpu.VMEM((channels, GRID, 2 * GRID), F32),
-            pltpu.VMEM((channels, GRID, 2 * GRID), F32),
-            pltpu.VMEM((channels, 2 * GRID, GRID), F32),
-            pltpu.VMEM((two, 2 * GRID, 2 * GRID), F32),
+            pltpu.VMEM((channels, PUPIL, GRID), F32),
+            pltpu.VMEM((channels, 2, GRID, GRID), F32),
+            pltpu.VMEM((channels, 2, GRID, GRID), F32),
+            pltpu.VMEM((channels, GRID, GRID), F32),
+            pltpu.VMEM((channels, 2, GRID, GRID), F32),
+            pltpu.VMEM((channels, 2, GRID, GRID), F32),
+            pltpu.VMEM((channels, 2, GRID, GRID), F32),
+            pltpu.VMEM((channels, 2, GRID, GRID), F32),
+            pltpu.VMEM((channels, 2, GRID, GRID), F32),
             pltpu.VMEM((n_chan, rows, PUPIL), F32),
             pltpu.VMEM((n_chan, rows, PUPIL), F32),
             pltpu.VMEM((PUPIL, PUPIL), F32),

time: 62.4 us -> 63 us (level)
  the two profiles are of different devices: /device:TPU:24 before, /device:TPU:8 now
where the time goes in v3:
time: 63 us; the launch traced here: 62.9 us
  Pallas kernels  61.1 us (97%)
  local copies, waits for them, and re-layouts  1.14 us (2%)
  between operations  0.64 us (1%)
    pallas_call x1, Pallas kernels, on_device(): pl.pallas_call(functools.partial(kernel, n_chan, channels, modes), out_sh...  61.1 us

profile of v3, /device:TPU:8, one launch (start us, length us, event | category | flops | bytes accessed | tf_op | source)
XLA Modules:
  0.0 62.9 jit_solution(1202437761167341539)
XLA Ops:
  0.6 61.1 %deconvolve.1 = (f32[4,2,8,256]{3,2,1,0:T(8,128)S(1)}, f32[1,36]{1,0:T(1,128)S(1)}) custom-call(f32[4,1,2,256,256]{4,3,2,1,0:T(8,128)} %images_hbm.1, f32[4,2,8,256]{3,2,1,0:T(8,128)} %objects_hbm.1, f32[1,36]{1,0:T(1,128)} %coeffs_hbm.1, f32[36,8,128]{2,1,0:T(8,128)} %maps_hbm.1, f32[128,128]{1,0:T(8,128)} %amp_hbm.1, f32[4]{0:T(128)} %scale_hbm.1, ...), custom_call_target="tpu_custom_call" | custom-call | tf_op jit(solution)/shard_map/deconvolve/pallas_call | solution.py:565
  61.8 0.6 %copy.11 = f32[4,2,8,256]{3,2,1,0:T(8,128)} copy(f32[4,2,8,256]{3,2,1,0:T(8,128)S(1)} %get-tuple-element.4) | data formatting | bytes 131072
  62.4 0.5 copy.12

commit v4 on v3

--- a/solution.py
+++ b/solution.py
@@ -3,7 +3,6 @@
 
 import jax
 import jax.numpy as jnp
-import ml_dtypes
 import numpy as np
 from jax import lax
 from jax.experimental import pallas as pl
@@ -37,11 +36,8 @@
         ],
         0,
     )
-    table = np.concatenate([first, second, left, herm, cos, sin, herm.T, back], 0).astype(np.float32)
-    high = table.astype(ml_dtypes.bfloat16)
-    high = high.astype(np.float32)
-    low = (table - high).astype(ml_dtypes.bfloat16).astype(np.float32)
-    return np.stack([high, low]).reshape(2, -1, GRID, GRID)
+    table = np.concatenate([first, second, left, herm, cos, sin, herm.T, back], 0)
+    return table.astype(np.float32).reshape(-1, GRID, GRID)
 
 
 def split(value):
@@ -169,7 +165,7 @@
 
     def local(k, src, dst):
         copy = pltpu.make_async_copy(src, dst, local_sem.at[k])
-        copy.start()
+        copy.start(priority=1)
         return copy
 
     maps_copy = local(0, maps_hbm, maps)
@@ -348,7 +344,7 @@
     tab_copy.wait()
 
     def table(k):
-        return tab[0, k].astype(BF16), tab[1, k].astype(BF16)
+        return split(tab[k])
 
     def each_channel(body):
         def run(j, carry):
@@ -357,12 +353,11 @@
 
         lax.fori_loop(0, channels, run, 0)
 
-    def each_half(body):
-        def run(i, carry):
-            body(lax.div(i, 2), lax.rem(i, 2))
-            return carry
-
-        lax.fori_loop(0, 2 * channels, run, 0)
+    def at_turn(j, turn, steps):
+        @pl.when(j == turn)
+        def _():
+            for step, which, stage in steps:
+                step(which, stage)
 
     wave = phases[...].reshape(PUPIL, PUPIL)
 
@@ -384,30 +379,32 @@
         half[j, 1, PUPIL:GRID, :] = -real
 
     each_channel(pupil_rows)
-    gather_next(0, 2)
-    gather_next(3, 2)
-
-    def to_spread(j, n):
-        spread[j, n] = dot3(*table(T_L2), *split(half[j, n]))
-
-    each_half(to_spread)
-    gather_next(1, 2)
-    gather_next(0, 3)
+
+    def to_spread(j):
+        l_hi, l_lo = table(T_L2)
+        for n in range(2):
+            spread[j, n] = dot3(l_hi, l_lo, *split(half[j, n]))
+        at_turn(j, 0, [(gather_next, 0, 2)])
+        at_turn(j, 1, [(gather_next, 1, 2), (gather_next, 3, 2)])
+        at_turn(j, 2, [(gather_next, 2, 2), (gather_next, 0, 3)])
+        at_turn(j, 3, [(gather_next, 1, 3)])
+
+    each_channel(to_spread)
 
     def fold(j):
         real, imag = spread[j, 0], spread[j, 1]
         folded[j] = dot3(*split((real * real + imag * imag) * inverse), *table(T_H))
+        at_turn(j, 1, [(gather_next, 3, 3)])
+        at_turn(j, 3, [(gather_next, 2, 3)])
 
     each_channel(fold)
-    gather_next(2, 2)
-    gather_next(1, 3)
-
-    def products(j, t):
-        product[j, t] = dot3(*table(T_C + t), *split(folded[j]))
-
-    each_half(products)
-    gather_next(3, 3)
-    gather_next(2, 3)
+
+    def products(j):
+        q_hi, q_lo = split(folded[j])
+        for t in range(2):
+            product[j, t] = dot3(*table(T_C + t), q_hi, q_lo)
+
+    each_channel(products)
     img_copy.wait()
 
     lane0 = lax.broadcasted_iota(jnp.int32, (16, PUPIL), 1) == 0
@@ -474,29 +471,30 @@
 
     lax.fori_loop(0, pairs, pair_residual, 0)
 
-    def unproducts(j, t):
-        back[j, t] = dot3(*table(T_C + t), *split(weight[j, t]))
-
-    each_half(unproducts)
-    reduce_next(0, 0)
+    def unproducts(j):
+        for t in range(2):
+            back[j, t] = dot3(*table(T_C + t), *split(weight[j, t]))
+        at_turn(j, 0, [(reduce_next, 0, 0)])
+        at_turn(j, 2, [(reduce_next, 1, 0), (reduce_next, 2, 0)])
+
+    each_channel(unproducts)
 
     def unfold(j):
         change = dot3(*split(back[j, 0] + back[j, 1]), *table(T_HT)) * (2.0 * inverse)
         along[j, 0] = change * spread[j, 0]
         along[j, 1] = change * spread[j, 1]
+        at_turn(j, 1, [(reduce_next, 0, 1)])
+        at_turn(j, 3, [(reduce_next, 1, 1), (reduce_next, 2, 1)])
 
     each_channel(unfold)
-    reduce_next(1, 0)
-    reduce_next(2, 0)
-    reduce_next(0, 1)
-
-    def from_spread(j, n):
-        last_rows[j, n] = dot3(*split(along[j, n]), *table(T_BACK + n))
-
-    each_half(from_spread)
-    reduce_next(1, 1)
-    reduce_next(2, 1)
-    reduce_next(0, 2)
+
+    def from_spread(j):
+        for n in range(2):
+            last_rows[j, n] = dot3(*split(along[j, n]), *table(T_BACK + n))
+        at_turn(j, 1, [(reduce_next, 0, 2)])
+        at_turn(j, 3, [(reduce_next, 1, 2), (reduce_next, 2, 2)])
+
+    each_channel(from_spread)
     pgrad[...] = jnp.zeros_like(pgrad)
 
     def to_pupil(j):
@@ -505,12 +503,12 @@
         g_i = g[PUPIL:GRID, 0:PUPIL] + g[0:PUPIL, PUPIL:GRID]
         change = scale[j] * (pupil[j, :, 0:PUPIL] * g_i - pupil[j, :, PUPIL:GRID] * g_r)
         pgrad[...] = pgrad[...] + change.reshape(pgrad.shape)
+        at_turn(j, 2, [(reduce_next, 0, 3)])
 
     each_channel(to_pupil)
     each_peer(lambda step: chan_copy(pgrad.at[peer(step)], land_pg.at[step], 1, peer(step)).start())
-    reduce_next(0, 3)
-    reduce_next(1, 2)
-    reduce_next(2, 2)
+    reduce_next(1, 3)
+    reduce_next(2, 3)
 
     part[...] = jnp.zeros_like(part)
     peers_wait(1, land_pg.at[others], False)
@@ -527,8 +525,6 @@
         preferred_element_type=F32,
     )
     each_peer(lambda step: chan_copy(vec, land_vec.at[step], 2, peer(step)).start())
-    reduce_next(1, 3)
-    reduce_next(2, 3)
     reduce_finish(0, 4)
     peers_wait(2, land_vec.at[others], False)
     answer = vec[...]
@@ -573,7 +569,7 @@
             pltpu.VMEM(mode_maps.shape, F32),
             pltpu.VMEM(amplitude.shape, F32),
             pltpu.VMEM(images.shape, F32),
-            pltpu.VMEM((2, 9, GRID, GRID), F32),
+            pltpu.VMEM((9, GRID, GRID), F32),
             pltpu.VMEM((channels, 32) + block, F32),
             pltpu.VMEM((channels, 32) + block, F32),
             pltpu.VMEM((channels, 16) + block, F32),

time: 63 us -> 63.9 us (1.014)
  Pallas kernels: 61.1 us -> 62 us
    pallas_call x1, Pallas kernels: 61.1 us -> 62 us  [on_device(): pl.pallas_call(functools.partial(kernel, n_chan, channels, modes), out_sh...]
where the time goes in v4:
time: 63.9 us; the launch traced here: 63.8 us
  Pallas kernels  62 us (97%)
  local copies, waits for them, and re-layouts  1.14 us (2%)
  between operations  0.64 us (1%)
    pallas_call x1, Pallas kernels, on_device(): pl.pallas_call(functools.partial(kernel, n_chan, channels, modes), out_sh...  62 us

profile of v4, /device:TPU:8, one launch (start us, length us, event | category | flops | bytes accessed | tf_op | source)
XLA Modules:
  0.0 63.8 jit_solution(351655957353282156)
XLA Ops:
  0.6 62.0 %deconvolve.1 = (f32[4,2,8,256]{3,2,1,0:T(8,128)S(1)}, f32[1,36]{1,0:T(1,128)S(1)}) custom-call(f32[4,1,2,256,256]{4,3,2,1,0:T(8,128)} %images_hbm.1, f32[4,2,8,256]{3,2,1,0:T(8,128)} %objects_hbm.1, f32[1,36]{1,0:T(1,128)} %coeffs_hbm.1, f32[36,8,128]{2,1,0:T(8,128)} %maps_hbm.1, f32[128,128]{1,0:T(8,128)} %amp_hbm.1, f32[4]{0:T(128)} %scale_hbm.1, ...), custom_call_target="tpu_custom_call" | custom-call | tf_op jit(solution)/shard_map/deconvolve/pallas_call | solution.py:561
  62.7 0.6 copy.11
  63.3 0.5 copy.12

commit v5 on v3

--- a/solution.py
+++ b/solution.py
@@ -159,10 +159,17 @@
 
     by_column = Order(cx, cy, (dev_xr, dev_xl, dev_yr, dev_yl))
     by_row = Order(cy, cx, (dev_yr, dev_yl, dev_xr, dev_xl))
-    last = channels - 1
+    first_pair = channels // 2
+
+    class Mixed:
+        pass
+
+    by_core = Mixed()
+    for name, value in vars(by_column).items():
+        setattr(by_core, name, cc * getattr(by_row, name) + (1 - cc) * value)
 
     def order(j):
-        return by_row if j == last else by_column
+        return by_column if j < first_pair else by_core
 
     def peer(step):
         return lax.rem(me + step, n_chan)
@@ -175,8 +182,8 @@
     maps_copy = local(0, maps_hbm, maps)
     coeffs_copy = local(1, coeffs_hbm, coeffs)
     obj_copies = [
-        local(2, objects_hbm.at[pl.ds(0, last)], obj.at[pl.ds(0, last), by_column.own]),
-        local(7, objects_hbm.at[last], obj.at[last, by_row.own]),
+        local(2, objects_hbm.at[pl.ds(0, 2)], obj.at[pl.ds(0, 2), by_column.own]),
+        local(7, objects_hbm.at[pl.ds(2, 2)], obj.at[pl.ds(2, 2), by_core.own]),
     ]
     scale_copy = local(3, scale_hbm, scale)
     amp_copy = local(4, amp_hbm, amp)
@@ -251,7 +258,7 @@
         gather_wait(j, stage)
         gather_start(j, stage + 1)
 
-    groups = ((0, 2), (2, 1), (3, 1))
+    groups = ((0, 2), (2, 2))
 
     def reduce_start(g, stage):
         first, count = groups[g]
@@ -328,7 +335,7 @@
 
     others = pl.ds(0, n_chan - 1)
     each_peer(lambda step: chan_copy(phases.at[me], phases.at[me], 0, peer(step)).start())
-    sequence = (3, 0, 1, 2)
+    sequence = (0, 2, 1, 3)
     for j in sequence:
         gather_start(j, 0)
 
@@ -385,13 +392,14 @@
 
     each_channel(pupil_rows)
     gather_next(0, 2)
-    gather_next(3, 2)
+    gather_next(2, 2)
 
     def to_spread(j, n):
         spread[j, n] = dot3(*table(T_L2), *split(half[j, n]))
 
     each_half(to_spread)
     gather_next(1, 2)
+    gather_next(3, 2)
     gather_next(0, 3)
 
     def fold(j):
@@ -399,7 +407,7 @@
         folded[j] = dot3(*split((real * real + imag * imag) * inverse), *table(T_H))
 
     each_channel(fold)
-    gather_next(2, 2)
+    gather_next(2, 3)
     gather_next(1, 3)
 
     def products(j, t):
@@ -407,7 +415,6 @@
 
     each_half(products)
     gather_next(3, 3)
-    gather_next(2, 3)
     img_copy.wait()
 
     lane0 = lax.broadcasted_iota(jnp.int32, (16, PUPIL), 1) == 0
@@ -416,9 +423,9 @@
         j = 2 * p + s
         at = pl.ds(pl.multiple_of(b * 16, 16), 16)
         crossed = lax.rem(b, 4) * 4 + lax.div(b, 4)
-        k = jnp.where(j == last, crossed, b) if s == 1 else b
-        o_r = jnp.concatenate([obj[j, k, 0], obj[j, k + 16, 0]], 0)
-        o_i = jnp.concatenate([obj[j, k, 1], obj[j, k + 16, 1]], 0)
+        k = 16 + p * crossed + (1 - p) * b
+        o_r = jnp.concatenate([obj[j, b, 0], obj[j, k, 0]], 0)
+        o_i = jnp.concatenate([obj[j, b, 1], obj[j, k, 1]], 0)
         p1, p3 = product[j, 0, at, 0:PUPIL], product[j, 0, at, PUPIL:GRID]
         p4, p2 = product[j, 1, at, 0:PUPIL], product[j, 1, at, PUPIL:GRID]
         t_r = jnp.concatenate(
@@ -431,10 +438,10 @@
         r_i = o_r * t_i + o_i * t_r - img[j, 0, 1, at, :]
         g_r = t_r * r_r + t_i * r_i
         g_i = t_r * r_i - t_i * r_r
-        term[j, k, 0] = g_r[0:8]
-        term[j, k + 16, 0] = g_r[8:16]
-        term[j, k, 1] = g_i[0:8]
-        term[j, k + 16, 1] = g_i[8:16]
+        term[j, b, 0] = g_r[0:8]
+        term[j, k, 0] = g_r[8:16]
+        term[j, b, 1] = g_i[0:8]
+        term[j, k, 1] = g_i[8:16]
         w_r = o_r * r_r + o_i * r_i
         w_i = o_r * r_i - o_i * r_r
         wr_p, wi_p = w_r[:, 0:PUPIL], w_i[:, 0:PUPIL]
@@ -468,7 +475,6 @@
         @pl.when(p == 1)
         def _():
             reduce_start(1, 0)
-            reduce_start(2, 0)
 
         return carry
 
@@ -487,7 +493,6 @@
 
     each_channel(unfold)
     reduce_next(1, 0)
-    reduce_next(2, 0)
     reduce_next(0, 1)
 
     def from_spread(j, n):
@@ -495,7 +500,6 @@
 
     each_half(from_spread)
     reduce_next(1, 1)
-    reduce_next(2, 1)
     reduce_next(0, 2)
     pgrad[...] = jnp.zeros_like(pgrad)
 
@@ -510,7 +514,6 @@
     each_peer(lambda step: chan_copy(pgrad.at[peer(step)], land_pg.at[step], 1, peer(step)).start())
     reduce_next(0, 3)
     reduce_next(1, 2)
-    reduce_next(2, 2)
 
     part[...] = jnp.zeros_like(part)
     peers_wait(1, land_pg.at[others], False)
@@ -528,7 +531,6 @@
     )
     each_peer(lambda step: chan_copy(vec, land_vec.at[step], 2, peer(step)).start())
     reduce_next(1, 3)
-    reduce_next(2, 3)
     reduce_finish(0, 4)
     peers_wait(2, land_vec.at[others], False)
     answer = vec[...]
@@ -536,7 +538,6 @@
         answer = answer + land_vec[step]
     mode_ref[...] = answer[0:1, 0:modes]
     reduce_finish(1, 4)
-    reduce_finish(2, 4)
 
     for j in range(channels):
         blocks = obj.at[j, pl.ds(0, 31)]

time: 63 us -> 62.1 us (0.986)
  Pallas kernels: 61.1 us -> 60.2 us
    pallas_call x1, Pallas kernels: 61.1 us -> 60.2 us  [on_device(): pl.pallas_call(functools.partial(kernel, n_chan, channels, modes), out_sh...]
where the time goes in v5:
time: 62.1 us; the launch traced here: 62 us
  Pallas kernels  60.2 us (97%)
  local copies, waits for them, and re-layouts  1.14 us (2%)
  between operations  0.64 us (1%)
    pallas_call x1, Pallas kernels, on_device(): pl.pallas_call(functools.partial(kernel, n_chan, channels, modes), out_sh...  60.2 us

profile of v5, /device:TPU:8, one launch (start us, length us, event | category | flops | bytes accessed | tf_op | source)
XLA Modules:
  0.0 62.0 jit_solution(2669816910034188075)
XLA Ops:
  0.6 60.2 %deconvolve.1 = (f32[4,2,8,256]{3,2,1,0:T(8,128)S(1)}, f32[1,36]{1,0:T(1,128)S(1)}) custom-call(f32[4,1,2,256,256]{4,3,2,1,0:T(8,128)} %images_hbm.1, f32[4,2,8,256]{3,2,1,0:T(8,128)} %objects_hbm.1, f32[1,36]{1,0:T(1,128)} %coeffs_hbm.1, f32[36,8,128]{2,1,0:T(8,128)} %maps_hbm.1, f32[128,128]{1,0:T(8,128)} %amp_hbm.1, f32[4]{0:T(128)} %scale_hbm.1, ...), custom_call_target="tpu_custom_call" | custom-call | tf_op jit(solution)/shard_map/deconvolve/pallas_call | solution.py:566
  60.8 0.6 %copy.11 = f32[4,2,8,256]{3,2,1,0:T(8,128)} copy(f32[4,2,8,256]{3,2,1,0:T(8,128)S(1)} %get-tuple-element.4) | data formatting | bytes 131072
  61.5 0.5 copy.12

commit v6 on v5

--- a/solution.py
+++ b/solution.py
@@ -159,8 +159,6 @@
 
     by_column = Order(cx, cy, (dev_xr, dev_xl, dev_yr, dev_yl))
     by_row = Order(cy, cx, (dev_yr, dev_yl, dev_xr, dev_xl))
-    first_pair = channels // 2
-
     class Mixed:
         pass
 
@@ -169,7 +167,7 @@
         setattr(by_core, name, cc * getattr(by_row, name) + (1 - cc) * value)
 
     def order(j):
-        return by_column if j < first_pair else by_core
+        return by_column if j == 0 else by_core
 
     def peer(step):
         return lax.rem(me + step, n_chan)
@@ -182,8 +180,8 @@
     maps_copy = local(0, maps_hbm, maps)
     coeffs_copy = local(1, coeffs_hbm, coeffs)
     obj_copies = [
-        local(2, objects_hbm.at[pl.ds(0, 2)], obj.at[pl.ds(0, 2), by_column.own]),
-        local(7, objects_hbm.at[pl.ds(2, 2)], obj.at[pl.ds(2, 2), by_core.own]),
+        local(2, objects_hbm.at[pl.ds(0, 1)], obj.at[pl.ds(0, 1), by_column.own]),
+        local(7, objects_hbm.at[pl.ds(1, 3)], obj.at[pl.ds(1, 3), by_core.own]),
     ]
     scale_copy = local(3, scale_hbm, scale)
     amp_copy = local(4, amp_hbm, amp)
@@ -258,7 +256,7 @@
         gather_wait(j, stage)
         gather_start(j, stage + 1)
 
-    groups = ((0, 2), (2, 2))
+    groups = ((0, 1), (1, 1), (2, 2))
 
     def reduce_start(g, stage):
         first, count = groups[g]
@@ -423,7 +421,7 @@
         j = 2 * p + s
         at = pl.ds(pl.multiple_of(b * 16, 16), 16)
         crossed = lax.rem(b, 4) * 4 + lax.div(b, 4)
-        k = 16 + p * crossed + (1 - p) * b
+        k = 16 + (crossed if s == 1 else p * crossed + (1 - p) * b)
         o_r = jnp.concatenate([obj[j, b, 0], obj[j, k, 0]], 0)
         o_i = jnp.concatenate([obj[j, b, 1], obj[j, k, 1]], 0)
         p1, p3 = product[j, 0, at, 0:PUPIL], product[j, 0, at, PUPIL:GRID]
@@ -471,10 +469,11 @@
         @pl.when(p == 0)
         def _():
             reduce_start(0, 0)
+            reduce_start(1, 0)
 
         @pl.when(p == 1)
         def _():
-            reduce_start(1, 0)
+            reduce_start(2, 0)
 
         return carry
 
@@ -485,6 +484,7 @@
 
     each_half(unproducts)
     reduce_next(0, 0)
+    reduce_next(1, 0)
 
     def unfold(j):
         change = dot3(*split(back[j, 0] + back[j, 1]), *table(T_HT)) * (2.0 * inverse)
@@ -492,15 +492,17 @@
         along[j, 1] = change * spread[j, 1]
 
     each_channel(unfold)
-    reduce_next(1, 0)
+    reduce_next(2, 0)
     reduce_next(0, 1)
+    reduce_next(1, 1)
 
     def from_spread(j, n):
         last_rows[j, n] = dot3(*split(along[j, n]), *table(T_BACK + n))
 
     each_half(from_spread)
-    reduce_next(1, 1)
+    reduce_next(2, 1)
     reduce_next(0, 2)
+    reduce_next(1, 2)
     pgrad[...] = jnp.zeros_like(pgrad)
 
     def to_pupil(j):
@@ -513,7 +515,8 @@
     each_channel(to_pupil)
     each_peer(lambda step: chan_copy(pgrad.at[peer(step)], land_pg.at[step], 1, peer(step)).start())
     reduce_next(0, 3)
-    reduce_next(1, 2)
+    reduce_next(1, 3)
+    reduce_next(2, 2)
 
     part[...] = jnp.zeros_like(part)
     peers_wait(1, land_pg.at[others], False)
@@ -530,14 +533,15 @@
         preferred_element_type=F32,
     )
     each_peer(lambda step: chan_copy(vec, land_vec.at[step], 2, peer(step)).start())
-    reduce_next(1, 3)
+    reduce_next(2, 3)
     reduce_finish(0, 4)
+    reduce_finish(1, 4)
     peers_wait(2, land_vec.at[others], False)
     answer = vec[...]
     for step in range(1, n_chan):
         answer = answer + land_vec[step]
     mode_ref[...] = answer[0:1, 0:modes]
-    reduce_finish(1, 4)
+    reduce_finish(2, 4)
 
     for j in range(channels):
         blocks = obj.at[j, pl.ds(0, 31)]

time: 62.1 us -> 61.3 us (0.987)
  the two profiles are of different devices: /device:TPU:8 before, /device:TPU:6 now
where the time goes in v6:
time: 61.3 us; the launch traced here: 61.1 us
  Pallas kernels  59.4 us (97%)
  local copies, waits for them, and re-layouts  1.14 us (2%)
  between operations  0.64 us (1%)
    pallas_call x1, Pallas kernels, on_device(): pl.pallas_call(functools.partial(kernel, n_chan, channels, modes), out_sh...  59.4 us

profile of v6, /device:TPU:6, one launch (start us, length us, event | category | flops | bytes accessed | tf_op | source)
XLA Modules:
  0.0 61.1 jit_solution(17418274638418759927)
XLA Ops:
  0.6 59.4 %deconvolve.1 = (f32[4,2,8,256]{3,2,1,0:T(8,128)S(1)}, f32[1,36]{1,0:T(1,128)S(1)}) custom-call(f32[4,1,2,256,256]{4,3,2,1,0:T(8,128)} %images_hbm.1, f32[4,2,8,256]{3,2,1,0:T(8,128)} %objects_hbm.1, f32[1,36]{1,0:T(1,128)} %coeffs_hbm.1, f32[36,8,128]{2,1,0:T(8,128)} %maps_hbm.1, f32[128,128]{1,0:T(8,128)} %amp_hbm.1, f32[4]{0:T(128)} %scale_hbm.1, ...), custom_call_target="tpu_custom_call" | custom-call | tf_op jit(solution)/shard_map/deconvolve/pallas_call | solution.py:570
  60.0 0.6 %copy.11 = f32[4,2,8,256]{3,2,1,0:T(8,128)} copy(f32[4,2,8,256]{3,2,1,0:T(8,128)S(1)} %get-tuple-element.4) | data formatting | bytes 131072
  60.6 0.5 copy.12
